TPU v7x, 256 devices: a whole 4x4x8 slice. The times are simulated.
256 devices in a mesh: pair: 2 (over core), seq: 32 (over y, z), tensor: 4 (over x).
Axes of the slice: x: 4, y: 4, z: 8, core: 2. Of those that a mesh axis runs over, the one named last changes fastest.
Arguments:
- latents: bfloat16 [2, 1, 8192, 1152], P('pair', None, 'seq'), may hold values from -36 to 36
- noise: bfloat16 [2, 1, 8192, 1152], P('pair', None, 'seq'), may hold values from -4 to 4
- timesteps: int32 [2, 1], P('pair'), may hold values from 50 to 949
- ref_losses: float32 [2, 1], replicated, may hold values from 0.5 to 2.5
- weights: bfloat16 [1152, 2, 4, 1152], P(None, None, None, 'tensor'), may hold values from -2.7 to 2.7
Outputs:
- dpo_loss: float32 [], replicated
- weight_grads: float32 [1152, 2, 4, 1152], P(('pair', 'seq'), None, None, 'tensor')
All inputs are finite; a program needn't handle non-finite values.
Results may differ from a plain program's by a relative error of at most 0.02.
Values may be sent and summed in bfloat16 or wider, within the bound.
A program may use at most 128 MiB of HBM per device.

v0:
```python
import math
import jax
import jax.numpy as jnp
from jax import lax
from jax.sharding import PartitionSpec as P

POSITIONS = 256
HEAD_DIM = 72
beta_dpo = 0.5
norm_eps = 1e-06


def layer_norm(hidden):
    center = hidden - jnp.mean(hidden, axis=-1, keepdims=True)
    inv_std = lax.rsqrt(jnp.mean(center * center, axis=-1, keepdims=True) + norm_eps)
    return (center * inv_std, inv_std)


def norm_backward(grad_norm, normed, inv_std):
    mean_grad = jnp.mean(grad_norm, axis=-1, keepdims=True)
    mean_prod = jnp.mean(grad_norm * normed, axis=-1, keepdims=True)
    return inv_std * (grad_norm - mean_grad - normed * mean_prod)


def attend_forward(queries, keyset, valueset):
    factor = HEAD_DIM ** (-0.5)
    scores = (
        jnp.einsum("bqhc,bkhc->bhqk", queries, keyset, preferred_element_type=jnp.float32) * factor
    )
    soft_weights = jax.nn.softmax(scores, axis=-1)
    rounded = soft_weights.astype(jnp.bfloat16)
    return jnp.einsum(
        "bhqk,bkhc->bqhc", rounded, valueset, preferred_element_type=jnp.float32
    ).astype(jnp.bfloat16)


def attend_backward(queries, keyset, valueset, grad_out):
    factor = HEAD_DIM ** (-0.5)
    scores = (
        jnp.einsum("bqhc,bkhc->bhqk", queries, keyset, preferred_element_type=jnp.float32) * factor
    )
    soft_weights = jax.nn.softmax(scores, axis=-1)
    rounded = soft_weights.astype(jnp.bfloat16)
    grad_value = jnp.einsum(
        "bhqk,bqhc->bkhc", rounded, grad_out, preferred_element_type=jnp.float32
    ).astype(jnp.bfloat16)
    grad_probs = jnp.einsum(
        "bqhc,bkhc->bhqk", grad_out, valueset, preferred_element_type=jnp.float32
    )
    delta_sum = jnp.sum(grad_probs * soft_weights, axis=-1, keepdims=True)
    grad_scores = (soft_weights * (grad_probs - delta_sum) * factor).astype(jnp.bfloat16)
    grad_query = jnp.einsum(
        "bhqk,bkhc->bqhc", grad_scores, keyset, preferred_element_type=jnp.float32
    ).astype(jnp.bfloat16)
    grad_key = jnp.einsum(
        "bhqk,bqhc->bkhc", grad_scores, queries, preferred_element_type=jnp.float32
    ).astype(jnp.bfloat16)
    return jnp.stack([grad_query, grad_key, grad_value], axis=2)


def heads_total(partial_rows):
    return lax.psum(partial_rows, "tensor")


def local(latents, noise, timesteps, ref_losses, weights):
    batch_count, row_count, model_width = (latents.shape[1], latents.shape[2], latents.shape[3])
    columns = weights.shape[3]
    heads_here = columns // HEAD_DIM
    frames_here = row_count // POSITIONS
    seq_count = lax.axis_size("seq")
    tokens_total = row_count * seq_count
    clean_rows = latents[0].astype(jnp.float32)
    target = noise[0].astype(jnp.float32)
    angle_value = (timesteps[0].astype(jnp.float32) / 1000.0 + 0.008) / 1.008 * (math.pi / 2)
    plan = (jnp.cos(angle_value) ** 2)[:, None, None]
    start_state = jnp.sqrt(plan) * clean_rows + jnp.sqrt(1.0 - plan) * target
    normed_one, inv_one = layer_norm(start_state)
    input_one = normed_one.astype(jnp.bfloat16)
    qkv_one = jnp.einsum(
        "btd,dje->btje", input_one, weights[:, 0, :3, :], preferred_element_type=jnp.float32
    ).astype(jnp.bfloat16)
    framed = qkv_one.reshape(batch_count * frames_here, POSITIONS, 3, heads_here, HEAD_DIM)
    attn_one = attend_forward(framed[:, :, 0], framed[:, :, 1], framed[:, :, 2]).reshape(
        batch_count, row_count, columns
    )
    state_one = start_state + heads_total(
        jnp.einsum("bte,de->btd", attn_one, weights[:, 0, 3, :], preferred_element_type=jnp.float32)
    )
    normed_two, inv_two = layer_norm(state_one)
    input_two = normed_two.astype(jnp.bfloat16)
    qkv_two = jnp.einsum(
        "btd,dje->btje", input_two, weights[:, 1, :3, :], preferred_element_type=jnp.float32
    ).astype(jnp.bfloat16)
    qkv_two = qkv_two.reshape(batch_count, frames_here, POSITIONS, 3, columns)
    piece = lax.all_to_all(qkv_two, "seq", split_axis=2, concat_axis=1, tiled=True)
    items = piece.shape[0]
    frames_all = piece.shape[1]
    piece_count = piece.shape[2]
    split_qkv = piece.reshape(items, frames_all, piece_count, 3, heads_here, HEAD_DIM).transpose(
        0, 2, 1, 3, 4, 5
    )
    split_qkv = split_qkv.reshape(items * piece_count, frames_all, 3, heads_here, HEAD_DIM)
    result = attend_forward(split_qkv[:, :, 0], split_qkv[:, :, 1], split_qkv[:, :, 2])
    result = result.reshape(items, piece_count, frames_all, columns).transpose(0, 2, 1, 3)
    attn_two = lax.all_to_all(result, "seq", split_axis=1, concat_axis=2, tiled=True).reshape(
        batch_count, row_count, columns
    )
    prediction = state_one + heads_total(
        jnp.einsum("bte,de->btd", attn_two, weights[:, 1, 3, :], preferred_element_type=jnp.float32)
    )
    diff_rows = prediction - target
    own_error = jnp.sum(diff_rows * diff_rows, axis=(1, 2))
    slot_mask = jnp.arange(2, dtype=jnp.int32) == lax.axis_index("pair")
    errors = lax.psum(jnp.where(slot_mask[:, None], own_error[None, :], 0.0), ("pair", "seq")) / (
        tokens_total * model_width
    )
    margin = errors[0] - ref_losses[0] - (errors[1] - ref_losses[1])
    dpo_loss = jnp.mean(jax.nn.softplus(beta_dpo * margin))
    signed = jnp.where(lax.axis_index("pair") == 0, 1.0, -1.0)
    coefficient = tokens_total * beta_dpo * jax.nn.sigmoid(beta_dpo * margin) * signed / batch_count
    grad_pred = coefficient[:, None, None] * 2.0 * diff_rows / model_width
    grad_two = grad_pred.astype(jnp.bfloat16)
    dout_two = jnp.einsum(
        "btd,de->bte", grad_two, weights[:, 1, 3, :], preferred_element_type=jnp.float32
    ).astype(jnp.bfloat16)
    dout_pos = lax.all_to_all(
        dout_two.reshape(batch_count, frames_here, POSITIONS, columns),
        "seq",
        split_axis=2,
        concat_axis=1,
        tiled=True,
    )
    frames_all, piece_count = (dout_pos.shape[1], dout_pos.shape[2])
    split_qkv = piece.reshape(
        batch_count, frames_all, piece_count, 3, heads_here, HEAD_DIM
    ).transpose(0, 2, 1, 3, 4, 5)
    split_qkv = split_qkv.reshape(batch_count * piece_count, frames_all, 3, heads_here, HEAD_DIM)
    split_grad = dout_pos.reshape(
        batch_count, frames_all, piece_count, heads_here, HEAD_DIM
    ).transpose(0, 2, 1, 3, 4)
    split_grad = split_grad.reshape(batch_count * piece_count, frames_all, heads_here, HEAD_DIM)
    dqkv_pos = attend_backward(
        split_qkv[:, :, 0], split_qkv[:, :, 1], split_qkv[:, :, 2], split_grad
    )
    dqkv_pos = dqkv_pos.reshape(batch_count, piece_count, frames_all, 3, columns).transpose(
        0, 2, 1, 3, 4
    )
    dqkv_two = lax.all_to_all(dqkv_pos, "seq", split_axis=1, concat_axis=2, tiled=True).reshape(
        batch_count, row_count, 3, columns
    )
    dnorm_two = heads_total(
        jnp.einsum(
            "btje,dje->btd", dqkv_two, weights[:, 1, :3, :], preferred_element_type=jnp.float32
        )
    )
    dstate = grad_pred + norm_backward(dnorm_two, normed_two, inv_two)
    grad_one = dstate.astype(jnp.bfloat16)
    dout_one = jnp.einsum(
        "btd,de->bte", grad_one, weights[:, 0, 3, :], preferred_element_type=jnp.float32
    ).astype(jnp.bfloat16)
    dout_framed = dout_one.reshape(batch_count * frames_here, POSITIONS, heads_here, HEAD_DIM)
    dqkv_one = attend_backward(
        framed[:, :, 0], framed[:, :, 1], framed[:, :, 2], dout_framed
    ).reshape(batch_count, row_count, 3, columns)
    flat_rows = batch_count * row_count
    input_one_flat = input_one.reshape(flat_rows, model_width)
    input_two_flat = input_two.reshape(flat_rows, model_width)
    grad_one_flat = grad_one.reshape(flat_rows, model_width)
    grad_two_flat = grad_two.reshape(flat_rows, model_width)
    dqkv_one_flat = dqkv_one.reshape(flat_rows, 3, columns)
    dqkv_two_flat = dqkv_two.reshape(flat_rows, 3, columns)
    attn_one_flat = attn_one.reshape(flat_rows, columns)
    attn_two_flat = attn_two.reshape(flat_rows, columns)
    first_block = jnp.concatenate(
        [
            jnp.einsum(
                "td,tje->dje", input_one_flat, dqkv_one_flat, preferred_element_type=jnp.float32
            ),
            jnp.einsum(
                "td,te->de", grad_one_flat, attn_one_flat, preferred_element_type=jnp.float32
            )[:, None],
        ],
        axis=1,
    )
    second_block = jnp.concatenate(
        [
            jnp.einsum(
                "td,tje->dje", input_two_flat, dqkv_two_flat, preferred_element_type=jnp.float32
            ),
            jnp.einsum(
                "td,te->de", grad_two_flat, attn_two_flat, preferred_element_type=jnp.float32
            )[:, None],
        ],
        axis=1,
    )
    grad_rows = lax.psum_scatter(
        jnp.stack([first_block, second_block], axis=1),
        ("pair", "seq"),
        scatter_dimension=0,
        tiled=True,
    )
    return (dpo_loss, grad_rows)


def solution(mesh):
    in_specs = (
        P("pair", None, "seq", None),
        P("pair", None, "seq", None),
        P("pair", None),
        P(),
        P(None, None, None, "tensor"),
    )
    out_specs = (P(), P(("pair", "seq"), None, None, "tensor"))
    return jax.shard_map(local, mesh=mesh, in_specs=in_specs, out_specs=out_specs, check_vma=False)
```

profile of v0, /device:TPU:2, one launch (start us, length us, event | category | flops | bytes accessed | tf_op | source)
XLA Modules:
  0.0 710.5 jit_solution(4275187458263335069)
XLA Ops:
  10.1 2.4 fusion.21
  14.8 2.7 convolution_bitcast_fusion.4
  17.6 54.2 %all-reduce.6.cloned.1.call-done = f32[1,256,1152]{2,1,0:T(8,128)} async-done(((f32[1,256,1152]{2,1,0:T(8,128)}), f32[1,256,1152]{2,1,0:T(8,128)}) %all-reduce.6.cloned.1.call-update) | async-done | bytes 1179664 | tf_op jit(solution)/shard_map/psum | solution.py:62
  73.7 3.2 fusion.31
  78.3 32.0 %all_to_all.16 = bf16[1,1,256,3,288]{4,3,1,0,2:T(4,128)(2,1)} all-to-all(bf16[1,1,256,3,288]{4,3,1,0,2:T(4,128)(2,1)S(1)} %copy.36), channel_id=1, replica_groups=mesh['pair'=2,'seq'=32,'tensor'=4] {'seq'}, dimensions={2} | all-to-all | bytes 884736 | tf_op jit(solution)/shard_map/all_to_all | solution.py:95
  110.3 2.6 reshape.512
  117.4 15.4 %all_to_all.17 = bf16[1,32,8,288]{3,2,0,1:T(8,128)(2,1)S(1)} all-to-all(bf16[1,32,8,288]{3,2,0,1:T(8,128)(2,1)S(1)} %copy.41), channel_id=1, replica_groups=mesh['pair'=2,'seq'=32,'tensor'=4] {'seq'}, dimensions={1} | all-to-all | bytes 294912 | tf_op jit(solution)/shard_map/all_to_all | solution.py:105
  133.4 2.6 convolution_bitcast_fusion.3
  136.8 45.7 %all-reduce.8.cloned.1.call-done = f32[1,256,1152]{2,1,0:T(8,128)} async-done(((f32[1,256,1152]{2,1,0:T(8,128)}), f32[1,256,1152]{2,1,0:T(8,128)}) %all-reduce.8.cloned.1.call-update) | async-done | bytes 1179664 | tf_op jit(solution)/shard_map/psum | solution.py:62
  182.5 2.2 multiply_reduce_fusion.1
  185.9 128.5 %psum.30 = f32[2,1]{0,1:T(1,128)} all-reduce(f32[2,1]{0,1:T(1,128)} %compare_select_fusion), channel_id=1, replica_groups=mesh['pair'=2,'seq'=32,'tensor'=4] {'pair','seq'}, use_global_device_ids=true, to_apply=%region_11.12 | all-reduce | flops 2 | bytes 16 | tf_op jit(solution)/shard_map/psum | solution.py:114
  322.7 3.3 reduce.15
  327.9 14.9 %all_to_all.18 = bf16[32,2,1152]{2,1,0:T(2,128)(2,1)} all-to-all(bf16[32,2,1152]{2,1,0:T(2,128)(2,1)} %reshape.515), channel_id=1, replica_groups=mesh['pair'=2,'seq'=32,'tensor'=4] {'seq'}, dimensions={0} | all-to-all | bytes 294912 | tf_op jit(solution)/shard_map/all_to_all | solution.py:126
  342.8 2.4 reshape.516
  345.2 2.8 bitcast_reduce_fusion
  351.9 2.7 fusion.42
  354.6 2.6 fusion.43
  371.8 23.3 %all_to_all.19 = bf16[1,32,8,3,288]{4,2,3,0,1:T(8,128)(2,1)S(1)} all-to-all(bf16[1,32,8,3,288]{4,2,3,0,1:T(8,128)(2,1)S(1)} %copy.48), channel_id=1, replica_groups=mesh['pair'=2,'seq'=32,'tensor'=4] {'seq'}, dimensions={1} | all-to-all | bytes 884736 | tf_op jit(solution)/shard_map/all_to_all | solution.py:148
  395.8 3.5 convolution_bitcast_fusion.2
  401.9 2.7 maximum_bitcast_fusion.1
  404.6 43.1 %all-reduce.10.cloned.1.call-done = f32[1,256,1152]{2,1,0:T(8,128)} async-done(((f32[1,256,1152]{2,1,0:T(8,128)}), f32[1,256,1152]{2,1,0:T(8,128)}) %all-reduce.10.cloned.1.call-update) | async-done | bytes 1179664 | tf_op jit(solution)/shard_map/psum | solution.py:62
  460.3 4.6 pad_maximum_fusion
  464.9 14.9 %copy.55 = f32[1152,2,4,288]{3,2,1,0:T(4,128)} copy(f32[1152,2,4,288]{0,3,2,1:T(8,128)} %pad_maximum_fusion) | data formatting | bytes 21233664 | tf_op jit(solution)/shard_map/stack | solution.py:197
  481.8 219.4 %all-reduce.12.cloned.1.call-done = f32[1152,2,4,288]{3,2,1,0:T(4,128)} async-done(((f32[1152,2,4,288]{3,2,1,0:T(4,128)}), f32[1152,2,4,288]{3,2,1,0:T(4,128)}) %all-reduce.12.cloned.1.call-update) | async-done | bytes 10616848
  (100 shorter events, 59.4 us)
Async XLA Ops:
  7.2 2.5 copy-start.1
  7.2 2.5 copy-start
  7.2 64.6 %all-reduce.6.cloned.1.call-start = ((), (), s32[]{:S(2)}) async-start(), calls=%async_computation.4 | async-start | bytes 2359296 | tf_op jit(solution)/shard_map/psum | solution.py:62
  12.5 2.3 copy-start.11
  14.1 0.7 copy-start.16
  14.8 2.7 copy-start.9
  17.6 165.0 %all-reduce.8.cloned.1.call-start = ((), (), s32[]{:S(2)}) async-start(), calls=%async_computation.5 | async-start | bytes 2359296 | tf_op jit(solution)/shard_map/psum | solution.py:62
  114.1 2.2 copy-start.8
  116.3 0.6 copy-start.15
  132.7 0.7 copy-start.7
  133.4 2.7 copy-start.13
  136.1 311.6 %all-reduce.10.cloned.1.call-start = ((), (), s32[]{:S(2)}) async-start(), calls=%async_computation.6 | async-start | bytes 2359296 | tf_op jit(solution)/shard_map/psum | solution.py:62
  395.0 0.8 copy-start.5
  399.3 301.9 %all-reduce.12.cloned.1.call-start = ((), (), s32[]{:S(2)}) async-start(), calls=%async_computation.7 | async-start | bytes 28311552
  399.6 1.4 copy-start.6
  447.6 1.7 copy-start.2
  449.8 2.1 copy-start.3
  449.8 1.7 copy-start.12
  449.8 2.1 copy-start.17
  456.1 1.1 copy-start.4
  456.1 1.1 copy-start.10
  457.6 2.2 slice-start
  458.5 1.8 slice-start.1
  479.8 0.7 copy-start.14
Sparse Core Ops, SparseCore 0:
  17.7 54.0 all-reduce.5
  136.2 46.3 all-reduce.7
  399.4 48.1 all-reduce.9
  479.9 221.2 all-reduce.11
where the time goes:
time: 712 us; the launch traced here: 711 us
  waiting for transfers between devices  362 us (51%)
  blocking collectives  214 us (30%)
  local copies, waits for them, and re-layouts  50.4 us (7%)
  matrix products  41.6 us (6%)
  other arithmetic  22.1 us (3%)
  between operations  19.5 us (3%)
    unnamed x5, waiting for transfers between devices  219 us
    psum x3, waiting for transfers between devices, heads_total(): return lax.psum(partial_rows, 'tensor')  143 us
    psum x1, blocking collectives, local(): lax.psum(jnp.where(slot_mask[:, None], own_error[None, :], 0.0), ('pair',...  128 us
    all_to_all x1, blocking collectives, local(): lax.all_to_all(qkv_two, 'seq', split_axis=2, concat_axis=1, tiled=True)  32 us
    all_to_all x1, blocking collectives, local(): lax.all_to_all(dqkv_pos, 'seq', split_axis=1, concat_axis=2, tiled=True)  23.3 us
    all_to_all x1, blocking collectives, local(): lax.all_to_all(result, 'seq', split_axis=1, concat_axis=2, tiled=True)  15.4 us
    another operation x1, local copies, waits for them, and re-layouts, local(): jnp.stack([first_block, second_block], axis=1)  14.9 us
    all_to_all x1, blocking collectives, local(): lax.all_to_all(dout_two.reshape(batch_count, frames_here, POSITIONS, colu...  14.9 us
  transfers between devices with their start and end apart: 4, of which 4 were waited for; matrix products, arithmetic and copies ran while one was open for 1% of the time, Pallas kernels for 0%

commit v1 on v0

--- a/solution.py
+++ b/solution.py
@@ -111,9 +111,9 @@
     diff_rows = prediction - target
     own_error = jnp.sum(diff_rows * diff_rows, axis=(1, 2))
     slot_mask = jnp.arange(2, dtype=jnp.int32) == lax.axis_index("pair")
-    errors = lax.psum(jnp.where(slot_mask[:, None], own_error[None, :], 0.0), ("pair", "seq")) / (
-        tokens_total * model_width
-    )
+    errors = lax.psum(
+        lax.psum(jnp.where(slot_mask[:, None], own_error[None, :], 0.0), "pair"), "seq"
+    ) / (tokens_total * model_width)
     margin = errors[0] - ref_losses[0] - (errors[1] - ref_losses[1])
     dpo_loss = jnp.mean(jax.nn.softplus(beta_dpo * margin))
     signed = jnp.where(lax.axis_index("pair") == 0, 1.0, -1.0)

time: 712 us -> 657 us (0.923)
  blocking collectives: 214 us -> 158 us
    psum x1 -> x2, blocking collectives: 128 us -> 78.7 us  [the longest x1 75.6 us: local(): lax.psum(lax.psum(jnp.where(slot_mask[:, None], own_error[None, :], 0.0),...]
where the time goes in v1:
time: 657 us; the launch traced here: 655 us
  waiting for transfers between devices  362 us (55%)
  blocking collectives  158 us (24%)
  local copies, waits for them, and re-layouts  50.4 us (8%)
  matrix products  41.6 us (6%)
  other arithmetic  22.1 us (3%)
  between operations  19.5 us (3%)
    unnamed x5, waiting for transfers between devices  219 us
    psum x3, waiting for transfers between devices, heads_total(): return lax.psum(partial_rows, 'tensor')  143 us
    psum x1, blocking collectives, local(): lax.psum(lax.psum(jnp.where(slot_mask[:, None], own_error[None, :], 0.0),...  75.6 us
    all_to_all x1, blocking collectives, local(): lax.all_to_all(qkv_two, 'seq', split_axis=2, concat_axis=1, tiled=True)  32 us
    all_to_all x1, blocking collectives, local(): lax.all_to_all(dqkv_pos, 'seq', split_axis=1, concat_axis=2, tiled=True)  17.6 us
    all_to_all x1, blocking collectives, local(): lax.all_to_all(result, 'seq', split_axis=1, concat_axis=2, tiled=True)  15.4 us
    another operation x1, local copies, waits for them, and re-layouts, local(): jnp.stack([first_block, second_block], axis=1)  14.9 us
    all_to_all x1, blocking collectives, local(): lax.all_to_all(dout_two.reshape(batch_count, frames_here, POSITIONS, colu...  14.9 us
  transfers between devices with their start and end apart: 4, of which 4 were waited for; matrix products, arithmetic and copies ran while one was open for 1% of the time, Pallas kernels for 0%

profile of v1, /device:TPU:2, one launch (start us, length us, event | category | flops | bytes accessed | tf_op | source)
XLA Modules:
  0.0 654.7 jit_solution(15983707954713036948)
XLA Ops:
  10.1 2.4 fusion.21
  14.8 2.7 convolution_bitcast_fusion.4
  17.6 54.2 %all-reduce.6.cloned.1.call-done = f32[1,256,1152]{2,1,0:T(8,128)} async-done(((f32[1,256,1152]{2,1,0:T(8,128)}), f32[1,256,1152]{2,1,0:T(8,128)}) %all-reduce.6.cloned.1.call-update) | async-done | bytes 1179664 | tf_op jit(solution)/shard_map/psum | solution.py:62
  73.7 3.2 fusion.31
  78.3 32.0 %all_to_all.16 = bf16[1,1,256,3,288]{4,3,1,0,2:T(4,128)(2,1)} all-to-all(bf16[1,1,256,3,288]{4,3,1,0,2:T(4,128)(2,1)S(1)} %copy.36), channel_id=1, replica_groups=mesh['pair'=2,'seq'=32,'tensor'=4] {'seq'}, dimensions={2} | all-to-all | bytes 884736 | tf_op jit(solution)/shard_map/all_to_all | solution.py:95
  110.3 2.6 reshape.512
  117.4 15.4 %all_to_all.17 = bf16[1,32,8,288]{3,2,0,1:T(8,128)(2,1)S(1)} all-to-all(bf16[1,32,8,288]{3,2,0,1:T(8,128)(2,1)S(1)} %copy.41), channel_id=1, replica_groups=mesh['pair'=2,'seq'=32,'tensor'=4] {'seq'}, dimensions={1} | all-to-all | bytes 294912 | tf_op jit(solution)/shard_map/all_to_all | solution.py:105
  133.4 2.6 convolution_bitcast_fusion.3
  136.8 45.7 %all-reduce.8.cloned.1.call-done = f32[1,256,1152]{2,1,0:T(8,128)} async-done(((f32[1,256,1152]{2,1,0:T(8,128)}), f32[1,256,1152]{2,1,0:T(8,128)}) %all-reduce.8.cloned.1.call-update) | async-done | bytes 1179664 | tf_op jit(solution)/shard_map/psum | solution.py:62
  185.9 3.1 psum.37
  189.0 75.6 %psum.38 = f32[2,1]{0,1:T(1,128)} all-reduce(f32[2,1]{0,1:T(1,128)} %psum.37), channel_id=1, replica_groups=mesh['pair'=2,'seq'=32,'tensor'=4] {'seq'}, use_global_device_ids=true, to_apply=%region_12.13 | all-reduce | flops 2 | bytes 16 | tf_op jit(solution)/shard_map/psum | solution.py:114
  272.9 3.3 reduce.15
  278.1 14.9 %all_to_all.18 = bf16[32,2,1152]{2,1,0:T(2,128)(2,1)} all-to-all(bf16[32,2,1152]{2,1,0:T(2,128)(2,1)} %reshape.515), channel_id=1, replica_groups=mesh['pair'=2,'seq'=32,'tensor'=4] {'seq'}, dimensions={0} | all-to-all | bytes 294912 | tf_op jit(solution)/shard_map/all_to_all | solution.py:126
  293.0 2.4 reshape.516
  295.3 2.8 bitcast_reduce_fusion
  302.0 2.7 fusion.42
  304.8 2.6 fusion.43
  321.9 17.6 %all_to_all.19 = bf16[1,32,8,3,288]{4,2,3,0,1:T(8,128)(2,1)S(1)} all-to-all(bf16[1,32,8,3,288]{4,2,3,0,1:T(8,128)(2,1)S(1)} %copy.48), channel_id=1, replica_groups=mesh['pair'=2,'seq'=32,'tensor'=4] {'seq'}, dimensions={1} | all-to-all | bytes 884736 | tf_op jit(solution)/shard_map/all_to_all | solution.py:148
  340.3 3.5 convolution_bitcast_fusion.2
  346.4 2.7 maximum_bitcast_fusion.1
  349.0 42.8 %all-reduce.10.cloned.1.call-done = f32[1,256,1152]{2,1,0:T(8,128)} async-done(((f32[1,256,1152]{2,1,0:T(8,128)}), f32[1,256,1152]{2,1,0:T(8,128)}) %all-reduce.10.cloned.1.call-update) | async-done | bytes 1179664 | tf_op jit(solution)/shard_map/psum | solution.py:62
  404.6 4.6 pad_maximum_fusion
  409.1 14.9 %copy.55 = f32[1152,2,4,288]{3,2,1,0:T(4,128)} copy(f32[1152,2,4,288]{0,3,2,1:T(8,128)} %pad_maximum_fusion) | data formatting | bytes 21233664 | tf_op jit(solution)/shard_map/stack | solution.py:197
  426.0 219.4 %all-reduce.12.cloned.1.call-done = f32[1152,2,4,288]{3,2,1,0:T(4,128)} async-done(((f32[1152,2,4,288]{3,2,1,0:T(4,128)}), f32[1152,2,4,288]{3,2,1,0:T(4,128)}) %all-reduce.12.cloned.1.call-update) | async-done | bytes 10616848
  (101 shorter events, 61.7 us)
Async XLA Ops:
  7.2 2.5 copy-start.1
  7.2 2.5 copy-start
  7.2 64.6 %all-reduce.6.cloned.1.call-start = ((), (), s32[]{:S(2)}) async-start(), calls=%async_computation.4 | async-start | bytes 2359296 | tf_op jit(solution)/shard_map/psum | solution.py:62
  12.5 2.3 copy-start.11
  14.1 0.7 copy-start.16
  14.8 2.7 copy-start.9
  17.6 165.0 %all-reduce.8.cloned.1.call-start = ((), (), s32[]{:S(2)}) async-start(), calls=%async_computation.5 | async-start | bytes 2359296 | tf_op jit(solution)/shard_map/psum | solution.py:62
  114.1 2.2 copy-start.8
  116.3 0.6 copy-start.15
  132.7 0.7 copy-start.7
  133.4 2.7 copy-start.13
  136.1 255.8 %all-reduce.10.cloned.1.call-start = ((), (), s32[]{:S(2)}) async-start(), calls=%async_computation.6 | async-start | bytes 2359296 | tf_op jit(solution)/shard_map/psum | solution.py:62
  339.5 0.8 copy-start.5
  343.8 301.6 %all-reduce.12.cloned.1.call-start = ((), (), s32[]{:S(2)}) async-start(), calls=%async_computation.7 | async-start | bytes 28311552
  344.1 1.4 copy-start.6
  391.9 1.7 copy-start.2
  394.1 2.1 copy-start.3
  394.1 1.7 copy-start.12
  394.1 2.1 copy-start.17
  400.4 1.1 copy-start.4
  400.4 1.1 copy-start.10
  401.8 2.2 slice-start
  402.7 1.8 slice-start.1
  424.0 0.7 copy-start.14
Sparse Core Ops, SparseCore 0:
  17.7 54.0 all-reduce.5
  136.2 46.3 all-reduce.7
  343.9 47.9 all-reduce.9
  424.2 221.1 all-reduce.11
